TPU v7x, 256 devices: a whole 4x4x8 slice. The times are simulated.
256 devices in a mesh: grp: 8 (over x, core), sec: 32 (over y, z).
Axes of the slice: x: 4, y: 4, z: 8, core: 2. Of those that a mesh axis runs over, the one named last changes fastest.
Arguments:
- left_env: bfloat16 [8, 2, 16384, 512], P('grp', None, 'sec'), may hold values from -0.09375 to 0.09375
- right_env: bfloat16 [8, 2, 16384, 512], P('grp', None, 'sec'), may hold values from -0.25 to 0.25
- guess: float32 [16384, 512], P('sec'), may hold values from -6 to 6
- precond: float32 [16384, 512], P('sec'), may hold values from 0.1 to 1
- sector_rows: int32 [32], P('sec'), may hold values from 128 to 512, as said below
Outputs:
- ritz_vector: float32 [16384, 512], P('sec')
- energies: float32 [3], replicated
Inputs may be any that keep to these rules, and one draw needn't show every extreme that they name: `sector_rows`: every entry is a multiple of 128; some sector uses all 512 rows.
All inputs are finite; a program needn't handle non-finite values.
Results may differ from a plain program's by a relative error of at most 0.02.
Values may be sent and summed in bfloat16 or wider, within the bound.
A program may use at most 64 MiB of HBM per device.

v0:
```python
import math

import jax
import jax.numpy as jnp
from jax import lax
from jax.sharding import PartitionSpec as P

ITERS = 3


def passed_along(block, axis, distance):
    devices = range(lax.axis_size(axis))
    route = [(i - distance, i) for i in devices if i - distance in devices]
    return lax.ppermute(block, axis, route)


def raise_term(left, right, vector):
    inner = jnp.dot(vector, right, preferred_element_type=jnp.float32).astype(jnp.bfloat16)
    return jnp.dot(left, inner, preferred_element_type=jnp.float32)


def lower_term(left, right, vector):
    inner = jnp.einsum("ij,kj->ik", vector, right, preferred_element_type=jnp.float32).astype(
        jnp.bfloat16
    )
    return jnp.einsum("ji,jk->ik", left, inner, preferred_element_type=jnp.float32)


def body(left_env, right_env, guess, precond, sector_rows):
    block = guess.shape[1]
    sectors = lax.axis_size("sec")
    used = sector_rows[0]
    left_own = left_env[0]
    right_own = right_env[0]
    row_ids = lax.iota(jnp.int32, block)
    col_ids = lax.iota(jnp.int32, block)
    mask = ((row_ids < used)[:, None] & (col_ids < used)[None, :]).astype(jnp.float32)

    def local_terms(pieces):
        own_vec = pieces[0]
        upper = pieces[1]
        partial_value = raise_term(left_own[0], right_own[0], own_vec) + lower_term(
            left_own[0], right_own[0], own_vec
        )
        raised = raise_term(left_own[1], right_own[1], own_vec)
        partial_value = partial_value + passed_along(raised.astype(jnp.bfloat16), "sec", 1).astype(
            raised.dtype
        )
        return partial_value + lower_term(left_own[1], right_own[1], upper)

    def operate(vector):
        rounded = vector.astype(jnp.bfloat16)
        upper = passed_along(rounded, "sec", -1)
        pieces = [rounded, upper]
        summed = lax.psum(local_terms(pieces).astype(jnp.bfloat16), "grp").astype(jnp.float32)
        return summed * mask

    def totals(values):
        return lax.psum(values, "sec")

    masked = mask * guess
    vector = masked / jnp.sqrt(totals(jnp.stack([jnp.sum(masked * masked)]))[0])
    image = operate(vector)
    ritz = totals(jnp.stack([jnp.sum(vector * image)]))[0]
    found = []
    for step in range(ITERS):
        resid = image - ritz * vector
        corr = precond * resid
        along = totals(jnp.stack([jnp.sum(vector * corr)]))[0]
        ortho = corr - along * vector
        normed = ortho / jnp.sqrt(totals(jnp.stack([jnp.sum(ortho * ortho)]))[0])
        image_two = operate(normed)
        pair = totals(jnp.stack([jnp.sum(normed * image), jnp.sum(normed * image_two)]))
        couple = pair[0]
        diag_two = pair[1]
        theta = (ritz + diag_two) / 2.0 - jnp.sqrt(((ritz - diag_two) / 2.0) ** 2 + couple**2)
        length = jnp.sqrt((diag_two - theta) ** 2 + couple**2)
        first_coef = (diag_two - theta) / length
        second_coef = -couple / length
        vector = first_coef * vector + second_coef * normed
        image = first_coef * image + second_coef * image_two
        ritz = theta
        found.append(theta)
    scaled = vector * math.sqrt(float(block * block * sectors))
    return (scaled, jnp.stack(found))


def solution(mesh):
    in_specs = (
        P("grp", None, "sec", None),
        P("grp", None, "sec", None),
        P("sec", None),
        P("sec", None),
        P("sec"),
    )
    out_specs = (P("sec", None), P())
    return jax.shard_map(body, mesh=mesh, in_specs=in_specs, out_specs=out_specs, check_vma=False)
```

profile of v0, /device:TPU:32, one launch (start us, length us, event | category | flops | bytes accessed | tf_op | source)
XLA Modules:
  0.0 1196.9 jit_solution(4838695191608270360)
XLA Ops:
  10.4 74.3 %psum.105 = f32[1]{0:T(128)} all-reduce(f32[1]{0:T(128)} %bitcast.1), channel_id=1, replica_groups=mesh['grp'=8,'sec'=32] {'sec'}, use_global_device_ids=true, to_apply=%region_1.0 | all-reduce | flops 1 | bytes 8 | tf_op jit(solution)/shard_map/psum | solution.py:59
  86.5 6.2 collective-permute-start.1
  92.7 2.8 fusion.8
  97.4 2.9 fusion.4
  100.3 3.2 fusion.3
  103.5 3.4 collective-permute-done
  106.9 3.2 add_convert_fusion.3
  110.1 60.5 %all-reduce.5.cloned.1.call-done = bf16[512,512]{0,1:T(8,128)(2,1)} async-done(((bf16[512,512]{0,1:T(8,128)(2,1)}), bf16[512,512]{0,1:T(8,128)(2,1)}) %all-reduce.5.cloned.1.call-update) | async-done | bytes 524304 | tf_op jit(solution)/shard_map/psum | solution.py:55
  174.4 72.3 %psum.107 = f32[]{:T(128)} all-reduce(f32[]{:T(128)} %multiply_reduce_fusion.11), channel_id=1, replica_groups=mesh['grp'=8,'sec'=32] {'sec'}, use_global_device_ids=true, to_apply=%region_4.0 | all-reduce | flops 1 | bytes 8 | tf_op jit(solution)/shard_map/psum | solution.py:59
  248.5 74.3 %psum.108 = f32[]{:T(128)} all-reduce(f32[]{:T(128)} %multiply_reduce_fusion.10), channel_id=1, replica_groups=mesh['grp'=8,'sec'=32] {'sec'}, use_global_device_ids=true, to_apply=%region_6.0 | all-reduce | flops 1 | bytes 8 | tf_op jit(solution)/shard_map/psum | solution.py:59
  322.8 2.6 multiply_reduce_fusion.9
  325.4 70.2 %psum.109 = f32[1]{0:T(128)} all-reduce(f32[1]{0:T(128)} %bitcast.10), channel_id=1, replica_groups=mesh['grp'=8,'sec'=32] {'sec'}, use_global_device_ids=true, to_apply=%region_8.0 | all-reduce | flops 1 | bytes 8 | tf_op jit(solution)/shard_map/psum | solution.py:59
  396.3 2.8 fusion.122
  399.1 2.9 fusion.9
  401.9 3.9 collective-permute-start.3
  407.8 3.1 fusion.5
  410.9 3.4 fusion.2
  414.2 3.0 collective-permute-done.2
  417.3 3.5 add_convert_fusion.2
  420.8 58.1 %all-reduce.7.cloned.1.call-done = bf16[512,512]{0,1:T(8,128)(2,1)} async-done(((bf16[512,512]{0,1:T(8,128)(2,1)}), bf16[512,512]{0,1:T(8,128)(2,1)}) %all-reduce.7.cloned.1.call-update) | async-done | bytes 524304 | tf_op jit(solution)/shard_map/psum | solution.py:55
  479.0 2.6 multiply_reduce_fusion.8
  482.9 71.6 %psum.111 = f32[2]{0:T(128)S(1)} all-reduce(f32[2]{0:T(128)S(1)} %pad_maximum_fusion), channel_id=1, replica_groups=mesh['grp'=8,'sec'=32] {'sec'}, use_global_device_ids=true, to_apply=%region_12.0 | all-reduce | flops 2 | bytes 16 | tf_op jit(solution)/shard_map/psum | solution.py:59
  560.5 3.6 multiply_reduce_fusion.6
  564.0 74.2 %psum.112 = f32[]{:T(128)} all-reduce(f32[]{:T(128)} %get-tuple-element.16), channel_id=1, replica_groups=mesh['grp'=8,'sec'=32] {'sec'}, use_global_device_ids=true, to_apply=%region_14.0 | all-reduce | flops 1 | bytes 8 | tf_op jit(solution)/shard_map/psum | solution.py:59
  638.3 3.3 multiply_reduce_fusion.5
  641.6 70.1 %psum.113 = f32[1]{0:T(128)} all-reduce(f32[1]{0:T(128)} %bitcast.20), channel_id=1, replica_groups=mesh['grp'=8,'sec'=32] {'sec'}, use_global_device_ids=true, to_apply=%region_16.0 | all-reduce | flops 1 | bytes 8 | tf_op jit(solution)/shard_map/psum | solution.py:59
  713.3 3.0 fusion.10
  716.4 3.9 collective-permute-start.5
  722.2 3.2 fusion.6
  725.5 3.6 fusion.1
  729.0 2.7 collective-permute-done.4
  731.7 3.5 add_convert_fusion.1
  735.3 58.1 %all-reduce.9.cloned.1.call-done = bf16[512,512]{0,1:T(8,128)(2,1)} async-done(((bf16[512,512]{0,1:T(8,128)(2,1)}), bf16[512,512]{0,1:T(8,128)(2,1)}) %all-reduce.9.cloned.1.call-update) | async-done | bytes 524304 | tf_op jit(solution)/shard_map/psum | solution.py:55
  797.1 71.6 %psum.115 = f32[2]{0:T(128)S(1)} all-reduce(f32[2]{0:T(128)S(1)} %pad_maximum_fusion.1), channel_id=1, replica_groups=mesh['grp'=8,'sec'=32] {'sec'}, use_global_device_ids=true, to_apply=%region_20.0 | all-reduce | flops 2 | bytes 16 | tf_op jit(solution)/shard_map/psum | solution.py:59
  873.0 3.8 multiply_reduce_fusion.2
  876.9 74.1 %psum.116 = f32[]{:T(128)} all-reduce(f32[]{:T(128)} %get-tuple-element.12), channel_id=1, replica_groups=mesh['grp'=8,'sec'=32] {'sec'}, use_global_device_ids=true, to_apply=%region_22.0 | all-reduce | flops 1 | bytes 8 | tf_op jit(solution)/shard_map/psum | solution.py:59
  950.9 3.6 multiply_reduce_fusion.1
  954.6 70.2 %psum.117 = f32[1]{0:T(128)} all-reduce(f32[1]{0:T(128)} %bitcast.30), channel_id=1, replica_groups=mesh['grp'=8,'sec'=32] {'sec'}, use_global_device_ids=true, to_apply=%region_24.0 | all-reduce | flops 1 | bytes 8 | tf_op jit(solution)/shard_map/psum | solution.py:59
  1026.4 2.9 fusion.11
  1029.3 3.9 collective-permute-start.7
  1035.1 3.1 fusion.7
  1038.2 3.4 fusion
  1041.6 3.0 collective-permute-done.6
  1044.6 3.3 add_convert_fusion
  1048.0 58.1 %all-reduce.11.cloned.1.call-done = bf16[512,512]{0,1:T(8,128)(2,1)} async-done(((bf16[512,512]{0,1:T(8,128)(2,1)}), bf16[512,512]{0,1:T(8,128)(2,1)}) %all-reduce.11.cloned.1.call-update) | async-done | bytes 524304 | tf_op jit(solution)/shard_map/psum | solution.py:55
  1106.1 2.7 multiply_reduce_fusion
  1110.1 71.6 %psum.119 = f32[2]{0:T(128)S(1)} all-reduce(f32[2]{0:T(128)S(1)} %pad_maximum_fusion.2), channel_id=1, replica_groups=mesh['grp'=8,'sec'=32] {'sec'}, use_global_device_ids=true, to_apply=%region_28.0 | all-reduce | flops 2 | bytes 16 | tf_op jit(solution)/shard_map/psum | solution.py:59
  1187.3 2.5 copy.11
  (46 shorter events, 29.0 us)
Async XLA Ops:
  7.2 163.5 %all-reduce.5.cloned.1.call-start = ((), (), s32[]{:S(2)}) async-start(), calls=%async_computation | async-start | bytes 1048576 | tf_op jit(solution)/shard_map/psum | solution.py:55
  9.4 83.3 %copy-start.5 = (bf16[1,2,512,512]{3,2,1,0:T(8,128)(2,1)S(1)}, bf16[1,2,512,512]{3,2,1,0:T(8,128)(2,1)}, u32[]{:S(2)}) copy-start(bf16[1,2,512,512]{3,2,1,0:T(8,128)(2,1)} %param.6) | copy-start | bytes 3145732
  10.4 82.3 %copy-start.3 = (bf16[1,2,512,512]{3,2,1,0:T(8,128)(2,1)S(1)}, bf16[1,2,512,512]{3,2,1,0:T(8,128)(2,1)}, u32[]{:S(2)}) copy-start(bf16[1,2,512,512]{3,2,1,0:T(8,128)(2,1)} %param.5) | copy-start | bytes 3145732
  86.5 20.4 %collective-permute-start.1 = (bf16[512,512]{0,1:T(8,128)(2,1)}, bf16[512,512]{0,1:T(8,128)(2,1)}, u32[]{:S(2)}, u32[]{:S(2)}) collective-permute-start(bf16[512,512]{0,1:T(8,128)(2,1)} %fusion.121), channel_id=1, source_target_pairs={{1,0},{2,1},{3,2},{4,3},{5,4},{6,5},{7,6},{8,7},{9,8},{10,9},{11,1... | collective-permute-start | bytes 1572872 | tf_op jit(solution)/shard_map/ppermute | solution.py:14
  95.5 11.4 collective-permute-start
  110.1 368.9 %all-reduce.7.cloned.1.call-start = ((), (), s32[]{:S(2)}) async-start(), calls=%async_computation.1 | async-start | bytes 1048576 | tf_op jit(solution)/shard_map/psum | solution.py:55
  172.8 73.9 %copy-start = (bf16[512,512]{0,1:T(8,128)(2,1)S(1)}, bf16[512,512]{0,1:T(8,128)(2,1)}, u32[]{:S(2)}) copy-start(bf16[512,512]{0,1:T(8,128)(2,1)} %all-reduce.5.cloned.1.call-done) | copy-start | bytes 1572868
  401.9 15.3 %collective-permute-start.3 = (bf16[512,512]{0,1:T(8,128)(2,1)S(1)}, bf16[512,512]{0,1:T(8,128)(2,1)}, u32[]{:S(2)}, u32[]{:S(2)}) collective-permute-start(bf16[512,512]{0,1:T(8,128)(2,1)S(1)} %get-tuple-element.18), channel_id=1, source_target_pairs={{1,0},{2,1},{3,2},{4,3},{5,4},{6,5},{7,6},{8,7},{9,8},{10,9},{11,1... | collective-permute-start | bytes 1572872 | tf_op jit(solution)/shard_map/ppermute | solution.py:14
  405.9 11.4 collective-permute-start.2
  420.8 372.7 %all-reduce.9.cloned.1.call-start = ((), (), s32[]{:S(2)}) async-start(), calls=%async_computation.2 | async-start | bytes 1048576 | tf_op jit(solution)/shard_map/psum | solution.py:55
  478.9 81.5 %copy-start.1 = (bf16[512,512]{0,1:T(8,128)(2,1)S(1)}, bf16[512,512]{0,1:T(8,128)(2,1)}, u32[]{:S(2)}) copy-start(bf16[512,512]{0,1:T(8,128)(2,1)} %all-reduce.7.cloned.1.call-done) | copy-start | bytes 1572868
  716.4 15.3 %collective-permute-start.5 = (bf16[512,512]{0,1:T(8,128)(2,1)}, bf16[512,512]{0,1:T(8,128)(2,1)}, u32[]{:S(2)}, u32[]{:S(2)}) collective-permute-start(bf16[512,512]{0,1:T(8,128)(2,1)} %fusion.119), channel_id=1, source_target_pairs={{1,0},{2,1},{3,2},{4,3},{5,4},{6,5},{7,6},{8,7},{9,8},{10,9},{11,1... | collective-permute-start | bytes 1572872 | tf_op jit(solution)/shard_map/ppermute | solution.py:14
  720.3 11.4 collective-permute-start.4
  735.2 370.8 %all-reduce.11.cloned.1.call-start = ((), (), s32[]{:S(2)}) async-start(), calls=%async_computation.3 | async-start | bytes 1048576 | tf_op jit(solution)/shard_map/psum | solution.py:55
  954.6 71.9 %copy-start.4 = (bf16[1,2,512,512]{3,2,1,0:T(8,128)(2,1)S(1)}, bf16[1,2,512,512]{3,2,1,0:T(8,128)(2,1)}, u32[]{:S(2)}) copy-start(bf16[1,2,512,512]{3,2,1,0:T(8,128)(2,1)} %param.5) | copy-start | bytes 3145732
  1029.3 15.3 %collective-permute-start.7 = (bf16[512,512]{0,1:T(8,128)(2,1)}, bf16[512,512]{0,1:T(8,128)(2,1)}, u32[]{:S(2)}, u32[]{:S(2)}) collective-permute-start(bf16[512,512]{0,1:T(8,128)(2,1)} %fusion.120), channel_id=1, source_target_pairs={{1,0},{2,1},{3,2},{4,3},{5,4},{6,5},{7,6},{8,7},{9,8},{10,9},{11,1... | collective-permute-start | bytes 1572872 | tf_op jit(solution)/shard_map/ppermute | solution.py:14
  1033.2 11.4 collective-permute-start.6
  1048.0 138.1 %copy-start.2 = (f32[512,512]{0,1:T(8,128)S(1)}, f32[512,512]{0,1:T(8,128)}, u32[]{:S(2)}) copy-start(f32[512,512]{0,1:T(8,128)} %get-tuple-element.13) | copy-start | bytes 3145732
Sparse Core Ops, SparseCore 0:
  110.2 60.4 all-reduce.4
  420.9 58.0 all-reduce.6
  735.4 58.0 all-reduce.8
  1048.1 57.9 all-reduce.10
where the time goes:
time: 1200 us
  blocking collectives  795 us (66%)
  waiting for transfers between devices  247 us (21%)
  matrix products  50.8 us (4%)
  other arithmetic  41 us (3%)
  between operations  30.2 us (3%)
  starting transfers between devices  25.9 us (2%)
    psum x11, blocking collectives, totals(): return lax.psum(values, 'sec')  795 us
    psum x4, waiting for transfers between devices, operate(): lax.psum(local_terms(pieces).astype(jnp.bfloat16), 'grp')  235 us
    dot_general x8, matrix products, lower_term(): jnp.einsum('ji,jk->ik', left, inner, preferred_element_type=jnp.float32)  27 us
    ppermute x8, starting transfers between devices, passed_along(): return lax.ppermute(block, axis, route)  25.7 us
  transfers between devices with their start and end apart: 12, of which 8 were waited for; matrix products, arithmetic and copies ran while one was open for 2% of the time, Pallas kernels for 0%

commit v1 on v0

v1 whole, which is shorter than its diff:
```python
import functools
import math

import jax
import jax.numpy as jnp
from jax import lax
from jax.experimental import pallas as pl
from jax.experimental.pallas import tpu as pltpu
from jax.sharding import PartitionSpec as P

ITERS = 3
B = 512
HALF = 256
Q = 128
NX = 4
NY = 4
MESH = pl.DeviceIdType.MESH
F32 = jnp.float32
BF16 = jnp.bfloat16


def rows_of(j):
    return pl.ds(pl.multiple_of(j * Q, Q), Q)


def dot(a, b):
    return jnp.dot(a, b, preferred_element_type=F32)


def fold(values):
    total = values[:, 0:128]
    for k in range(1, values.shape[1] // 128):
        total = total + values[:, k * 128 : (k + 1) * 128]
    return jnp.sum(total, axis=0, keepdims=True)


def kernel(
    sectors, ny, nz,
    left, right, guess, precond, used_ref,
    out, energies,
    lr, lo, rt, ru, rraw,
    kw, kw16, kup, xsend,
    x, h, t, xu, hu, tu, tb, tub,
    gown, gup, so, sr, ro, rr,
    acc, praise, in1, inn, keep_own,
    sc_c, sc_x, sc_y, sc_z, coef,
    load_sem, env_s, env_r, k_s, k_r,
    up_s, up_r, upc_s, upc_r, own_s, own_r, ownc_s, ownc_r,
    so_s, ro_r, sr_s, rr_r,
    scc_s, scc_r, scx_s, scx_r, scy_s, scy_r, scz_s, scz_r,
):
    g = lax.axis_index("grp")
    s = lax.axis_index("sec")
    px, c = g // 2, g % 2
    py, pz = s // nz, s % nz
    above = lax.rem(s + 1, sectors)
    below = lax.rem(s + sectors - 1, sectors)
    other = 1 - c
    partner = (px * 2 + other, s)
    mine = pl.ds(pl.multiple_of(c * HALF, HALF), HALF)
    theirs = pl.ds(pl.multiple_of(other * HALF, HALF), HALF)

    def xdev(j, sec):
        return (j * 2 + c, sec)

    def xoff(k):
        return lax.rem(px + k, NX)

    def rcopy(src, dst, ssem, rsem, dev):
        return pltpu.make_async_remote_copy(
            src_ref=src, dst_ref=dst, send_sem=ssem, recv_sem=rsem, device_id=dev, device_id_type=MESH
        )

    loads = [
        (right.at[0, 1, :, mine], rt.at[:, 0:256]),
        (left.at[0, 1], lr.at[:, 0:512]),
        (right.at[0, 0, :, mine], rt.at[:, 512:768]),
        (left.at[0, 0], lo.at[:, 0:512]),
        (right.at[0, 0, mine, :], rraw.at[0]),
        (right.at[0, 1, mine, :], rraw.at[2]),
        (guess.at[:, 0:256], t.at[0]),
        (guess.at[:, 256:512], t.at[1]),
        (precond.at[:, 0:256], kw.at[0]),
        (precond.at[:, 256:512], kw.at[1]),
    ]
    local = [pltpu.make_async_copy(a, b, load_sem.at[i]) for i, (a, b) in enumerate(loads)]
    for i in (6, 7, 1, 0, 3, 2, 4, 5, 8, 9):
        local[i].start()

    barrier = pltpu.get_barrier_semaphore()
    peers = [partner]
    peers += [xdev(xoff(k), s) for k in range(1, NX)]
    peers += [xdev(xoff(k), above) for k in range(NX)]
    peers += [xdev(xoff(k), below) for k in range(NX)]
    peers += [(g, lax.rem(py + k, ny) * nz + pz) for k in range(1, ny)]
    peers += [(g, py * nz + lax.rem(pz + k, nz)) for k in range(1, nz)]
    for peer in peers:
        pl.semaphore_signal(barrier, inc=1, device_id=peer, device_id_type=MESH)

    used = used_ref[0]
    row_ids = lax.broadcasted_iota(jnp.int32, (Q, HALF), 0)
    col_ids = lax.broadcasted_iota(jnp.int32, (Q, HALF), 1)

    def mask_of(j, half):
        return ((row_ids + j * Q < used) & (col_ids + half * HALF < used)).astype(F32)

    local[6].wait()
    local[7].wait()

    def start_rows(j, _):
        for half in range(2):
            value = t[half, rows_of(j)] * mask_of(j, half)
            t[half, rows_of(j)] = value
            x[half, rows_of(j)] = jnp.zeros((Q, HALF), F32)
            h[half, rows_of(j)] = jnp.zeros((Q, HALF), F32)
            rounded = value.astype(BF16)
            tb[rows_of(j), half * HALF : (half + 1) * HALF] = rounded
            xsend[half, rows_of(j)] = rounded
        return 0

    lax.fori_loop(0, NX, start_rows, 0)
    pl.semaphore_wait(barrier, len(peers))

    def up_start(j, _):
        rcopy(
            xsend.at[c, rows_of(j)], gup.at[0, c, rows_of(j)], up_s.at[0, j], up_r.at[0, j], (g, below)
        ).start()
        return 0

    lax.fori_loop(0, NX, up_start, 0)
    envs = [
        (left.at[0, 1], lr.at[:, 512:1024]),
        (right.at[0, 1, :, theirs], rt.at[:, 256:512]),
        (left.at[0, 0], lo.at[:, 512:1024]),
        (right.at[0, 0, :, theirs], rt.at[:, 768:1024]),
        (right.at[0, 0, theirs, :], rraw.at[1]),
        (right.at[0, 1, theirs, :], rraw.at[3]),
    ]
    env = [rcopy(a, b, env_s.at[i], env_r.at[i], partner) for i, (a, b) in enumerate(envs)]
    for copy in env:
        copy.start()

    for i in (0, 1, 2, 3, 4, 5, 8, 9):
        local[i].wait()

    def k_rows(j, _):
        for half in range(2):
            kw16[half, rows_of(j)] = kw[half, rows_of(j)].astype(BF16)
        return 0

    lax.fori_loop(0, NX, k_rows, 0)
    k_copy = rcopy(kw16, kup, k_s, k_r, (g, below))

    has_above = (s < sectors - 1).astype(F32)

    def gate(values):
        return (values.astype(F32) * has_above).astype(BF16)

    lo[:, 1024:1536] = lo[:, 0:512].T
    lo[:, 2048:2560] = lr[:, 0:512].T
    rt[:, 0:256] = gate(rt[:, 0:256])
    rt[:, 1024:1280] = rraw[0].T
    ru[:, 0:256] = gate(rraw[2].T)
    for copy in env:
        copy.wait_recv()
    lo[:, 1536:2048] = lo[:, 512:1024].T
    lo[:, 2560:3072] = lr[:, 512:1024].T
    rt[:, 256:512] = gate(rt[:, 256:512])
    rt[:, 1280:1536] = rraw[1].T
    ru[:, 256:512] = gate(rraw[3].T)

    def upper_forward(r):
        def one(j, _):
            rcopy(
                gup.at[r, c, rows_of(j)], gup.at[r, c, rows_of(j)], up_s.at[r, j], up_r.at[r, j], partner
            ).wait_recv()
            rcopy(
                gup.at[r, c, rows_of(j)], gup.at[r, c, rows_of(j)], upc_s.at[r, j], upc_r.at[r, j], partner
            ).start()
            return 0

        lax.fori_loop(0, NX, one, 0)

    def upper_update(r):
        def wait(j):
            rcopy(
                gup.at[r, c, rows_of(j)], gup.at[r, other, rows_of(j)], upc_s.at[r, j], upc_r.at[r, j], partner
            ).wait_recv()

        @pl.when(r == 0)
        def _():
            def one(j, _):
                wait(j)
                for half in range(2):
                    got = gup[0, half, rows_of(j)]
                    tub[rows_of(j), half * HALF : (half + 1) * HALF] = got
                    tu[half, rows_of(j)] = got.astype(F32)
                    xu[half, rows_of(j)] = jnp.zeros((Q, HALF), F32)
                    hu[half, rows_of(j)] = jnp.zeros((Q, HALF), F32)
                return 0

            lax.fori_loop(0, NX, one, 0)
            k_copy.start()

        @pl.when(r == 1)
        def _():
            k_copy.wait_recv()

        @pl.when(r > 0)
        def _():
            a0, d0, ritz = coef[0], coef[1], coef[2]

            def one(j, _):
                wait(j)
                for half in range(2):
                    new_x = a0 * xu[half, rows_of(j)] + d0 * tu[half, rows_of(j)]
                    new_h = a0 * hu[half, rows_of(j)] + d0 * gup[r, half, rows_of(j)].astype(F32)
                    new_t = kup[half, rows_of(j)].astype(F32) * (new_h - ritz * new_x)
                    xu[half, rows_of(j)] = new_x
                    hu[half, rows_of(j)] = new_h
                    tu[half, rows_of(j)] = new_t
                    tub[rows_of(j), half * HALF : (half + 1) * HALF] = new_t.astype(BF16)
                return 0

            lax.fori_loop(0, NX, one, 0)

    def local_sums(extra):
        xb, tv, hb = x[c, rows_of(px)], t[c, rows_of(px)], h[c, rows_of(px)]
        return jnp.concatenate(
            [
                fold(xb * tv), fold(tv * tv), fold(tv * hb), extra,
                fold(xb * xb), fold(xb * hb), jnp.zeros((2, 128), F32),
            ],
            axis=0,
        )

    def stage(buf, ssem, rsem, size, me, dev_of):
        def send(r, value):
            buf[r, me] = value
            for k in range(1, size):
                rcopy(
                    buf.at[r, me], buf.at[r, me], ssem.at[r, k], rsem.at[r, me], dev_of(lax.rem(me + k, size))
                ).start()

        def finish(r):
            for k in range(1, size):
                src = lax.rem(me + k, size)
                rcopy(buf.at[r, me], buf.at[r, src], ssem.at[r, k], rsem.at[r, src], dev_of(src)).wait_recv()
            total = buf[r, 0]
            for k in range(1, size):
                total = total + buf[r, k]
            return total

        def drain(r):
            for k in range(1, size):
                rcopy(
                    buf.at[r, me], buf.at[r, me], ssem.at[r, k], rsem.at[r, me], dev_of(lax.rem(me + k, size))
                ).wait_send()

        return send, finish, drain

    c_send, c_finish, c_drain = stage(sc_c, scc_s, scc_r, 2, c, lambda i: (px * 2 + i, s))
    x_send, x_finish, x_drain = stage(sc_x, scx_s, scx_r, NX, px, lambda i: (i * 2 + c, s))
    y_send, y_finish, y_drain = stage(sc_y, scy_s, scy_r, ny, py, lambda i: (g, i * nz + pz))
    z_send, z_finish, z_drain = stage(sc_z, scz_s, scz_r, nz, pz, lambda i: (g, py * nz + i))

    def coefficients(total, r, ritz):
        sums = jnp.sum(total, axis=1, keepdims=True)
        xt, tt, th, tat, xx, xh = (sums[k : k + 1, 0:1] for k in range(6))
        norm = jnp.sqrt(tt)
        start = (jnp.zeros_like(norm), 1.0 / norm, tat / tt)
        n2 = tt - 2.0 * xt * xt + xt * xt * xx
        n = jnp.sqrt(n2)
        couple = (th - xt * xh) / n
        diag = (tat - 2.0 * xt * th + xt * xt * xh) / n2
        theta = (ritz + diag) / 2.0 - jnp.sqrt(((ritz - diag) / 2.0) ** 2 + couple**2)
        length = jnp.sqrt((diag - theta) ** 2 + couple**2)
        first = (diag - theta) / length
        second = -couple / length
        later = (first - second * xt / n, second / n, theta)
        return [jnp.where(r == 0, u, v) for u, v in zip(start, later)]

    def set_coef(total, r, ritz):
        a0, d0, new = coefficients(total, r, ritz)
        coef[0] = a0[0, 0]
        coef[1] = d0[0, 0]
        coef[2] = new[0, 0]
        return new

    def raise_inner():
        inner = dot(tb[...], rt[:, 0:512])
        in1[0:512] = inner[:, 0:256].astype(BF16)
        in1[512:1024] = inner[:, 256:512].astype(BF16)

    def round_body(r, ritz):
        raise_inner()

        def raise_rows(k, _):
            j = xoff(k + 2)
            value = dot(lr[rows_of(j)], in1[...])
            praise[rows_of(j)] = value
            sr[r, rows_of(j)] = value.astype(BF16)
            rcopy(sr.at[r, rows_of(j)], rr.at[r, px], sr_s.at[r, j], rr_r.at[r, px], xdev(j, above)).start()
            return 0

        lax.fori_loop(0, NX, raise_rows, 0)
        upper_forward(r)

        for k in range(4):
            inn[k * 512 : (k + 1) * 512] = dot(tb[...], rt[:, 512 + k * 256 : 768 + k * 256]).astype(BF16)

        def own_rows(j, part):
            value = dot(lo[rows_of(j), 0:2048], inn[0:2048])
            acc[rows_of(j)] = value
            return part + fold(value * t[c, rows_of(j)])

        part = lax.fori_loop(0, NX, own_rows, jnp.zeros((1, 128), F32))

        upper_update(r)
        for k in range(2):
            inn[2048 + k * 512 : 2560 + k * 512] = dot(tub[...], ru[:, k * 256 : (k + 1) * 256]).astype(BF16)

        def raise_part(j, total):
            return total + 2.0 * fold(praise[rows_of(j)] * tu[c, rows_of(j)])

        part = lax.fori_loop(0, NX, raise_part, part)
        c_send(r, local_sums(part))

        def lower_rows(k, _):
            j = xoff(k + 2)
            value = acc[rows_of(j)] + dot(lo[rows_of(j), 2048:3072], inn[2048:3072])

            @pl.when(j == px)
            def _():
                keep_own[...] = value

            @pl.when(j != px)
            def _():
                so[r, rows_of(j)] = value.astype(BF16)
                rcopy(so.at[r, rows_of(j)], ro.at[r, px], so_s.at[r, j], ro_r.at[r, px], xdev(j, s)).start()

            return 0

        lax.fori_loop(0, NX, lower_rows, 0)
        x_send(r, c_finish(r))

        def raised_in(j, _):
            rcopy(sr.at[r, rows_of(j)], rr.at[r, j], sr_s.at[r, j], rr_r.at[r, j], xdev(j, below)).wait_recv()
            return 0

        def own_in(k, _):
            j = xoff(k)
            rcopy(so.at[r, rows_of(j)], ro.at[r, j], so_s.at[r, j], ro_r.at[r, j], xdev(j, s)).wait_recv()
            return 0

        y_send(r, x_finish(r))
        lax.fori_loop(1, NX, own_in, 0)
        value = keep_own[...]
        for k in range(1, NX):
            value = value + ro[r, xoff(k)].astype(F32)
        lax.fori_loop(0, NX, raised_in, 0)
        for k in range(NX):
            value = value + rr[r, k].astype(F32)
        block = (value * mask_of(px, c)).astype(BF16)
        gown[r, c, rows_of(px)] = block

        home = gown.at[r, c, rows_of(px)]
        rcopy(home, home, ownc_s.at[r, px], ownc_r.at[r, px], partner).start()
        for k in (2, 1, 3):
            j = xoff(k)
            rcopy(home, home, own_s.at[r, k], own_r.at[r, px], xdev(j, s)).start()
        for k in (2, 1, 3, 0):
            j = xoff(k)
            rcopy(
                home, gup.at[r + 1, c, rows_of(px)], up_s.at[r + 1, k], up_r.at[r + 1, px], xdev(j, below)
            ).start()

        z_send(r, y_finish(r))

        for k in (1, 3, 2):
            there = gown.at[r, c, rows_of(xoff(k))]
            rcopy(there, there, own_s.at[r, k], own_r.at[r, xoff(k)], partner).wait_recv()
            rcopy(there, there, ownc_s.at[r, xoff(k)], ownc_r.at[r, xoff(k)], partner).start()

        new_ritz = set_coef(z_finish(r), r, ritz)

        @pl.when(r > 0)
        def _():
            energies[r - 1] = coef[2]

        a0, d0, theta = coef[0], coef[1], coef[2]

        def update(k, _):
            j = xoff(k)
            there = gown.at[r, other, rows_of(j)]
            rcopy(there, there, ownc_s.at[r, j], ownc_r.at[r, j], partner).wait_recv()
            for half in range(2):
                new_x = a0 * x[half, rows_of(j)] + d0 * t[half, rows_of(j)]
                new_h = a0 * h[half, rows_of(j)] + d0 * gown[r, half, rows_of(j)].astype(F32)
                new_t = kw[half, rows_of(j)] * (new_h - theta * new_x)
                x[half, rows_of(j)] = new_x
                h[half, rows_of(j)] = new_h
                t[half, rows_of(j)] = new_t
                tb[rows_of(j), half * HALF : (half + 1) * HALF] = new_t.astype(BF16)
            return 0

        lax.fori_loop(0, NX, update, 0)
        return new_ritz

    ritz = lax.fori_loop(0, ITERS, round_body, jnp.zeros((1, 1), F32))

    last = ITERS
    raise_inner()
    inn[0:512] = dot(tb[...], rt[:, 512:768]).astype(BF16)
    inn[512:1024] = dot(tb[...], rt[:, 768:1024]).astype(BF16)

    def last_rows(j, part):
        praise[rows_of(j)] = dot(lr[rows_of(j)], in1[...])
        return part + 2.0 * fold(dot(lo[rows_of(j), 0:1024], inn[0:1024]) * t[c, rows_of(j)])

    part = lax.fori_loop(0, NX, last_rows, jnp.zeros((1, 128), F32))
    upper_forward(last)
    upper_update(last)

    def last_part(j, total):
        return total + 2.0 * fold(praise[rows_of(j)] * tu[c, rows_of(j)])

    part = lax.fori_loop(0, NX, last_part, part)
    c_send(last, local_sums(part))
    x_send(last, c_finish(last))

    def drain_round(r, _):
        def rows(j, _):
            rcopy(sr.at[r, rows_of(j)], rr.at[r, px], sr_s.at[r, j], rr_r.at[r, px], xdev(j, above)).wait_send()
            home = gown.at[r, c, rows_of(px)]
            rcopy(home, home, ownc_s.at[r, j], ownc_r.at[r, px], partner).wait_send()
            return 0

        def others(k, _):
            j = xoff(k)
            rcopy(so.at[r, rows_of(j)], ro.at[r, px], so_s.at[r, j], ro_r.at[r, px], xdev(j, s)).wait_send()
            home = gown.at[r, c, rows_of(px)]
            rcopy(home, home, own_s.at[r, k], own_r.at[r, px], xdev(j, s)).wait_send()
            return 0

        lax.fori_loop(0, NX, rows, 0)
        lax.fori_loop(1, NX, others, 0)
        return 0

    def drain_upper(r, _):
        def rows(j, _):
            there = gup.at[r, c, rows_of(j)]
            rcopy(there, there, up_s.at[r, j], up_r.at[r, j], (g, below)).wait_send()
            rcopy(there, there, upc_s.at[r, j], upc_r.at[r, j], partner).wait_send()
            return 0

        lax.fori_loop(0, NX, rows, 0)
        return 0

    lax.fori_loop(0, ITERS, drain_round, 0)
    lax.fori_loop(0, ITERS + 1, drain_upper, 0)
    for copy in env:
        copy.wait_send()
    k_copy.wait_send()

    y_send(last, x_finish(last))
    z_send(last, y_finish(last))
    set_coef(z_finish(last), last, ritz)
    energies[last - 1] = coef[2]
    scale = math.sqrt(float(B * B * sectors))
    a0, d0 = coef[0] * scale, coef[1] * scale

    def write(j, _):
        for half in range(2):
            out[rows_of(j), half * HALF : (half + 1) * HALF] = a0 * x[half, rows_of(j)] + d0 * t[half, rows_of(j)]
        return 0

    lax.fori_loop(0, NX, write, 0)

    def drain_sums(r, _):
        for drain in (c_drain, x_drain, y_drain, z_drain):
            drain(r)
        return 0

    lax.fori_loop(0, ITERS + 1, drain_sums, 0)


def body(left_env, right_env, guess, precond, sector_rows):
    sectors = lax.axis_size("sec")
    ny = min(NY, sectors)
    nz = sectors // ny
    rounds = ITERS + 1
    vm, dma = pltpu.VMEM, pltpu.SemaphoreType.DMA
    halves = (2, B, HALF)
    scratch = [
        vm((B, 1024), BF16), vm((B, 3072), BF16), vm((B, 1536), BF16), vm((B, 512), BF16), vm((4, HALF, B), BF16),
        vm(halves, F32), vm(halves, BF16), vm(halves, BF16), vm(halves, BF16),
        vm(halves, F32), vm(halves, F32), vm(halves, F32), vm(halves, F32), vm(halves, F32), vm(halves, F32),
        vm((B, B), BF16), vm((B, B), BF16),
        vm((ITERS,) + halves, BF16), vm((rounds,) + halves, BF16),
        vm((ITERS, B, HALF), BF16), vm((ITERS, B, HALF), BF16),
        vm((ITERS, NX, Q, HALF), BF16), vm((ITERS, NX, Q, HALF), BF16),
        vm((B, HALF), F32), vm((B, HALF), F32), vm((1024, HALF), BF16), vm((3072, HALF), BF16), vm((Q, HALF), F32),
        vm((rounds, 2, 8, 128), F32), vm((rounds, NX, 8, 128), F32),
        vm((rounds, ny, 8, 128), F32), vm((rounds, nz, 8, 128), F32),
        pltpu.SMEM((4,), F32),
        dma((10,)), dma((6,)), dma((6,)), dma, dma,
        dma((rounds, NX)), dma((rounds, NX)), dma((rounds, NX)), dma((rounds, NX)),
        dma((ITERS, NX)), dma((ITERS, NX)), dma((ITERS, NX)), dma((ITERS, NX)),
        dma((ITERS, NX)), dma((ITERS, NX)), dma((ITERS, NX)), dma((ITERS, NX)),
        dma((rounds, 2)), dma((rounds, 2)), dma((rounds, NX)), dma((rounds, NX)),
        dma((rounds, ny)), dma((rounds, ny)), dma((rounds, nz)), dma((rounds, nz)),
    ]
    any_space = pl.BlockSpec(memory_space=pl.ANY)
    return pl.pallas_call(
        functools.partial(kernel, sectors, ny, nz),
        out_shape=(jax.ShapeDtypeStruct((B, B), F32), jax.ShapeDtypeStruct((ITERS,), F32)),
        in_specs=[any_space] * 4 + [pl.BlockSpec(memory_space=pltpu.SMEM)],
        out_specs=(pl.BlockSpec(memory_space=pltpu.VMEM), pl.BlockSpec(memory_space=pltpu.SMEM)),
        scratch_shapes=scratch,
        compiler_params=pltpu.CompilerParams(
            collective_id=0, has_side_effects=True, vmem_limit_bytes=56 * 1024 * 1024
        ),
        name="davidson",
    )(left_env, right_env, guess, precond, sector_rows)


def solution(mesh):
    in_specs = (
        P("grp", None, "sec", None),
        P("grp", None, "sec", None),
        P("sec", None),
        P("sec", None),
        P("sec"),
    )
    out_specs = (P("sec", None), P())
    return jax.shard_map(body, mesh=mesh, in_specs=in_specs, out_specs=out_specs, check_vma=False)
```

time: 1200 us -> 106 us (0.09)
  blocking collectives: 795 us -> 0 us
  waiting for transfers between devices: 247 us -> 0 us
  Pallas kernels: 0 us -> 102 us
  matrix products: 50.8 us -> 0 us
  other arithmetic: 41 us -> 0 us
  between operations: 30.2 us -> 1.29 us
  starting transfers between devices: 25.9 us -> 0 us
    psum x11 -> x0, blocking collectives: 795 us -> none  [totals(): return lax.psum(values, 'sec')]
    psum x4 -> x0, waiting for transfers between devices: 235 us -> none  [operate(): lax.psum(local_terms(pieces).astype(jnp.bfloat16), 'grp')]
    pallas_call x0 -> x1, Pallas kernels: none -> 102 us  [body(): pl.pallas_call(functools.partial(kernel, sectors, ny, nz), out_shape=(jax...]
    dot_general x16 -> x0, matrix products: 50.8 us -> none  [the longest x8 27 us: lower_term(): jnp.einsum('ji,jk->ik', left, inner, preferred_element_type=jnp.float32)]
    reduce_sum x11 -> x0, other arithmetic: 29.5 us -> none  [the longest x3 9.49 us: body(): normed = ortho / jnp.sqrt(totals(jnp.stack([jnp.sum(ortho * ortho)]))[0])]
    ppermute x8 -> x0, starting transfers between devices: 25.7 us -> none  [passed_along(): return lax.ppermute(block, axis, route)]
    ppermute x8 -> x0, waiting for transfers between devices: 12.1 us -> none  [passed_along(): return lax.ppermute(block, axis, route)]
  transfers between devices with their start and end apart: 12 -> 0, of which waited for: 8 -> 0; matrix products, arithmetic and copies ran while one was open for 2% -> 0% of each run, Pallas kernels for 0% -> 0%
where the time goes in v1:
time: 106 us
  Pallas kernels  102 us (96%)
  local copies, waits for them, and re-layouts  2.78 us (3%)
  between operations  1.29 us (1%)
    pallas_call x1, Pallas kernels, body(): pl.pallas_call(functools.partial(kernel, sectors, ny, nz), out_shape=(jax...  102 us
    unnamed x4, local copies, waits for them, and re-layouts  2.78 us

profile of v1, /device:TPU:32, one launch (start us, length us, event | category | flops | bytes accessed | tf_op | source)
XLA Modules:
  0.0 105.9 jit_solution(12550342087276519635)
XLA Ops:
  1.3 101.8 %davidson.1 = (f32[512,512]{1,0:T(8,128)}, f32[3]{0:T(128)}) custom-call(bf16[1,2,512,512]{3,2,1,0:T(8,128)(2,1)} %left.1, bf16[1,2,512,512]{3,2,1,0:T(8,128)(2,1)} %right.1, f32[512,512]{1,0:T(8,128)} %guess.1, f32[512,512]{1,0:T(8,128)} %precond.1, s32[1]{0:T(128)S(6)} %copy.9.used_ref), custom_call_target="tpu_custom_call" | custom-call | tf_op jit(solution)/shard_map/davidson/pallas_call | solution.py:515
  103.1 0.0 copy-start
  103.1 2.3 %copy.10 = f32[512,512]{1,0:T(8,128)} copy(f32[512,512]{1,0:T(8,128)} %get-tuple-element.4) | data formatting | bytes 2097152
  105.4 0.0 copy-done
  105.4 0.5 copy.11
Async XLA Ops:
  103.1 2.3 %copy-start = (f32[3]{0:T(128)S(1)}, f32[3]{0:T(128)}, u32[]{:S(2)}) copy-start(f32[3]{0:T(128)} %get-tuple-element.5) | copy-start | bytes 40

commit v2 on v1

--- a/solution.py
+++ b/solution.py
@@ -90,8 +90,7 @@
     barrier = pltpu.get_barrier_semaphore()
     peers = [partner]
     peers += [xdev(xoff(k), s) for k in range(1, NX)]
-    peers += [xdev(xoff(k), above) for k in range(NX)]
-    peers += [xdev(xoff(k), below) for k in range(NX)]
+    peers += [(g, above), (g, below)]
     peers += [(g, lax.rem(py + k, ny) * nz + pz) for k in range(1, ny)]
     peers += [(g, py * nz + lax.rem(pz + k, nz)) for k in range(1, nz)]
     for peer in peers:
@@ -140,34 +139,45 @@
     for copy in env:
         copy.start()
 
-    for i in (0, 1, 2, 3, 4, 5, 8, 9):
-        local[i].wait()
-
-    def k_rows(j, _):
-        for half in range(2):
-            kw16[half, rows_of(j)] = kw[half, rows_of(j)].astype(BF16)
-        return 0
-
-    lax.fori_loop(0, NX, k_rows, 0)
-    k_copy = rcopy(kw16, kup, k_s, k_r, (g, below))
+    k_copy = rcopy(kw16.at[c], kup.at[c], k_s.at[0], k_r.at[0], (g, below))
+    k_forward = rcopy(kup.at[c], kup.at[c], k_s.at[1], k_r.at[1], partner)
 
     has_above = (s < sectors - 1).astype(F32)
 
     def gate(values):
         return (values.astype(F32) * has_above).astype(BF16)
 
-    lo[:, 1024:1536] = lo[:, 0:512].T
-    lo[:, 2048:2560] = lr[:, 0:512].T
-    rt[:, 0:256] = gate(rt[:, 0:256])
-    rt[:, 1024:1280] = rraw[0].T
-    ru[:, 0:256] = gate(rraw[2].T)
-    for copy in env:
-        copy.wait_recv()
-    lo[:, 1536:2048] = lo[:, 512:1024].T
-    lo[:, 2560:3072] = lr[:, 512:1024].T
-    rt[:, 256:512] = gate(rt[:, 256:512])
-    rt[:, 1280:1536] = rraw[1].T
-    ru[:, 256:512] = gate(rraw[3].T)
+    def ready_raise():
+        local[0].wait()
+        local[1].wait()
+        env[0].wait_recv()
+        env[1].wait_recv()
+        rt[:, 0:512] = gate(rt[:, 0:512])
+
+    def ready_own():
+        for i in (2, 3, 4):
+            local[i].wait()
+        rt[:, 1024:1280] = rraw[0].T
+        lo[:, 1024:1536] = lo[:, 0:512].T
+        for i in (2, 3, 4):
+            env[i].wait_recv()
+        rt[:, 1280:1536] = rraw[1].T
+        lo[:, 1536:2048] = lo[:, 512:1024].T
+
+    def ready_lower():
+        local[5].wait()
+        ru[:, 0:256] = gate(rraw[2].T)
+        lo[:, 2048:2560] = lr[:, 0:512].T
+        env[5].wait_recv()
+        ru[:, 256:512] = gate(rraw[3].T)
+        lo[:, 2560:3072] = lr[:, 512:1024].T
+
+    def ready_weights():
+        local[8].wait()
+        local[9].wait()
+        for half in range(2):
+            kw16[half] = kw[half].astype(BF16)
+        k_copy.start()
 
     def upper_forward(r):
         def one(j, _):
@@ -200,11 +210,10 @@
                 return 0
 
             lax.fori_loop(0, NX, one, 0)
-            k_copy.start()
 
         @pl.when(r == 1)
         def _():
-            k_copy.wait_recv()
+            rcopy(kup.at[other], kup.at[other], k_s.at[1], k_r.at[1], partner).wait_recv()
 
         @pl.when(r > 0)
         def _():
@@ -293,42 +302,60 @@
         in1[512:1024] = inner[:, 256:512].astype(BF16)
 
     def round_body(r, ritz):
+        @pl.when(r == 0)
+        def _():
+            ready_raise()
+
         raise_inner()
+        praise[...] = dot(lr[...], in1[...])
 
         def raise_rows(k, _):
             j = xoff(k + 2)
-            value = dot(lr[rows_of(j)], in1[...])
-            praise[rows_of(j)] = value
-            sr[r, rows_of(j)] = value.astype(BF16)
-            rcopy(sr.at[r, rows_of(j)], rr.at[r, px], sr_s.at[r, j], rr_r.at[r, px], xdev(j, above)).start()
+            sr[r, rows_of(j)] = praise[rows_of(j)].astype(BF16)
+            rcopy(sr.at[r, rows_of(j)], rr.at[r, rows_of(j)], sr_s.at[r, j], rr_r.at[r, j], (g, above)).start()
             return 0
 
         lax.fori_loop(0, NX, raise_rows, 0)
-        upper_forward(r)
+
+        @pl.when(r == 0)
+        def _():
+            ready_own()
 
         for k in range(4):
             inn[k * 512 : (k + 1) * 512] = dot(tb[...], rt[:, 512 + k * 256 : 768 + k * 256]).astype(BF16)
-
-        def own_rows(j, part):
-            value = dot(lo[rows_of(j), 0:2048], inn[0:2048])
-            acc[rows_of(j)] = value
-            return part + fold(value * t[c, rows_of(j)])
-
-        part = lax.fori_loop(0, NX, own_rows, jnp.zeros((1, 128), F32))
+        upper_forward(r)
+        acc[...] = dot(lo[:, 0:2048], inn[0:2048])
+
+        def own_part(j, total):
+            return total + fold(acc[rows_of(j)] * t[c, rows_of(j)])
+
+        part = lax.fori_loop(0, NX, own_part, jnp.zeros((1, 128), F32))
+
+        @pl.when(r == 0)
+        def _():
+            ready_lower()
 
         upper_update(r)
+
+        def raise_part(j, total):
+            return total + 2.0 * fold(praise[rows_of(j)] * tu[c, rows_of(j)])
+
+        part = lax.fori_loop(0, NX, raise_part, part)
+        c_send(r, local_sums(part))
+
+        @pl.when(r == 0)
+        def _():
+            ready_weights()
+
         for k in range(2):
             inn[2048 + k * 512 : 2560 + k * 512] = dot(tub[...], ru[:, k * 256 : (k + 1) * 256]).astype(BF16)
-
-        def raise_part(j, total):
-            return total + 2.0 * fold(praise[rows_of(j)] * tu[c, rows_of(j)])
-
-        part = lax.fori_loop(0, NX, raise_part, part)
-        c_send(r, local_sums(part))
-
-        def lower_rows(k, _):
+        acc[...] += dot(lo[:, 2048:3072], inn[2048:3072])
+        x_send(r, c_finish(r))
+
+        def send_rows(k, _):
             j = xoff(k + 2)
-            value = acc[rows_of(j)] + dot(lo[rows_of(j), 2048:3072], inn[2048:3072])
+            rcopy(sr.at[r, rows_of(j)], rr.at[r, rows_of(j)], sr_s.at[r, j], rr_r.at[r, j], (g, above)).wait_recv()
+            value = acc[rows_of(j)] + rr[r, rows_of(j)].astype(F32)
 
             @pl.when(j == px)
             def _():
@@ -341,12 +368,7 @@
 
             return 0
 
-        lax.fori_loop(0, NX, lower_rows, 0)
-        x_send(r, c_finish(r))
-
-        def raised_in(j, _):
-            rcopy(sr.at[r, rows_of(j)], rr.at[r, j], sr_s.at[r, j], rr_r.at[r, j], xdev(j, below)).wait_recv()
-            return 0
+        lax.fori_loop(0, NX, send_rows, 0)
 
         def own_in(k, _):
             j = xoff(k)
@@ -358,9 +380,6 @@
         value = keep_own[...]
         for k in range(1, NX):
             value = value + ro[r, xoff(k)].astype(F32)
-        lax.fori_loop(0, NX, raised_in, 0)
-        for k in range(NX):
-            value = value + rr[r, k].astype(F32)
         block = (value * mask_of(px, c)).astype(BF16)
         gown[r, c, rows_of(px)] = block
 
@@ -369,18 +388,21 @@
         for k in (2, 1, 3):
             j = xoff(k)
             rcopy(home, home, own_s.at[r, k], own_r.at[r, px], xdev(j, s)).start()
-        for k in (2, 1, 3, 0):
+        rcopy(home, gup.at[r + 1, c, rows_of(px)], up_s.at[r + 1, px], up_r.at[r + 1, px], (g, below)).start()
+
+        @pl.when(r == 0)
+        def _():
+            k_copy.wait_recv()
+            k_forward.start()
+
+        z_send(r, y_finish(r))
+
+        for k in (1, 3, 2):
             j = xoff(k)
-            rcopy(
-                home, gup.at[r + 1, c, rows_of(px)], up_s.at[r + 1, k], up_r.at[r + 1, px], xdev(j, below)
-            ).start()
-
-        z_send(r, y_finish(r))
-
-        for k in (1, 3, 2):
-            there = gown.at[r, c, rows_of(xoff(k))]
-            rcopy(there, there, own_s.at[r, k], own_r.at[r, xoff(k)], partner).wait_recv()
-            rcopy(there, there, ownc_s.at[r, xoff(k)], ownc_r.at[r, xoff(k)], partner).start()
+            there = gown.at[r, c, rows_of(j)]
+            rcopy(there, there, own_s.at[r, k], own_r.at[r, j], partner).wait_recv()
+            rcopy(there, there, ownc_s.at[r, j], ownc_r.at[r, j], partner).start()
+            rcopy(there, gup.at[r + 1, c, rows_of(j)], up_s.at[r + 1, j], up_r.at[r + 1, j], (g, below)).start()
 
         new_ritz = set_coef(z_finish(r), r, ritz)
 
@@ -414,12 +436,14 @@
     inn[0:512] = dot(tb[...], rt[:, 512:768]).astype(BF16)
     inn[512:1024] = dot(tb[...], rt[:, 768:1024]).astype(BF16)
 
-    def last_rows(j, part):
-        praise[rows_of(j)] = dot(lr[rows_of(j)], in1[...])
-        return part + 2.0 * fold(dot(lo[rows_of(j), 0:1024], inn[0:1024]) * t[c, rows_of(j)])
-
-    part = lax.fori_loop(0, NX, last_rows, jnp.zeros((1, 128), F32))
     upper_forward(last)
+    praise[...] = dot(lr[...], in1[...])
+    acc[...] = dot(lo[:, 0:1024], inn[0:1024])
+
+    def last_own(j, part):
+        return part + 2.0 * fold(acc[rows_of(j)] * t[c, rows_of(j)])
+
+    part = lax.fori_loop(0, NX, last_own, jnp.zeros((1, 128), F32))
     upper_update(last)
 
     def last_part(j, total):
@@ -431,7 +455,7 @@
 
     def drain_round(r, _):
         def rows(j, _):
-            rcopy(sr.at[r, rows_of(j)], rr.at[r, px], sr_s.at[r, j], rr_r.at[r, px], xdev(j, above)).wait_send()
+            rcopy(sr.at[r, rows_of(j)], rr.at[r, rows_of(j)], sr_s.at[r, j], rr_r.at[r, j], (g, above)).wait_send()
             home = gown.at[r, c, rows_of(px)]
             rcopy(home, home, ownc_s.at[r, j], ownc_r.at[r, px], partner).wait_send()
             return 0
@@ -462,13 +486,13 @@
     for copy in env:
         copy.wait_send()
     k_copy.wait_send()
+    k_forward.wait_send()
 
     y_send(last, x_finish(last))
     z_send(last, y_finish(last))
     set_coef(z_finish(last), last, ritz)
     energies[last - 1] = coef[2]
-    scale = math.sqrt(float(B * B * sectors))
-    a0, d0 = coef[0] * scale, coef[1] * scale
+    a0, d0 = coef[0], coef[1]
 
     def write(j, _):
         for half in range(2):
@@ -499,12 +523,12 @@
         vm((B, B), BF16), vm((B, B), BF16),
         vm((ITERS,) + halves, BF16), vm((rounds,) + halves, BF16),
         vm((ITERS, B, HALF), BF16), vm((ITERS, B, HALF), BF16),
-        vm((ITERS, NX, Q, HALF), BF16), vm((ITERS, NX, Q, HALF), BF16),
+        vm((ITERS, NX, Q, HALF), BF16), vm((ITERS, B, HALF), BF16),
         vm((B, HALF), F32), vm((B, HALF), F32), vm((1024, HALF), BF16), vm((3072, HALF), BF16), vm((Q, HALF), F32),
         vm((rounds, 2, 8, 128), F32), vm((rounds, NX, 8, 128), F32),
         vm((rounds, ny, 8, 128), F32), vm((rounds, nz, 8, 128), F32),
         pltpu.SMEM((4,), F32),
-        dma((10,)), dma((6,)), dma((6,)), dma, dma,
+        dma((10,)), dma((6,)), dma((6,)), dma((2,)), dma((2,)),
         dma((rounds, NX)), dma((rounds, NX)), dma((rounds, NX)), dma((rounds, NX)),
         dma((ITERS, NX)), dma((ITERS, NX)), dma((ITERS, NX)), dma((ITERS, NX)),
         dma((ITERS, NX)), dma((ITERS, NX)), dma((ITERS, NX)), dma((ITERS, NX)),
@@ -512,7 +536,7 @@
         dma((rounds, ny)), dma((rounds, ny)), dma((rounds, nz)), dma((rounds, nz)),
     ]
     any_space = pl.BlockSpec(memory_space=pl.ANY)
-    return pl.pallas_call(
+    vector, energies = pl.pallas_call(
         functools.partial(kernel, sectors, ny, nz),
         out_shape=(jax.ShapeDtypeStruct((B, B), F32), jax.ShapeDtypeStruct((ITERS,), F32)),
         in_specs=[any_space] * 4 + [pl.BlockSpec(memory_space=pltpu.SMEM)],
@@ -523,6 +547,7 @@
         ),
         name="davidson",
     )(left_env, right_env, guess, precond, sector_rows)
+    return vector * math.sqrt(float(B * B * sectors)), energies
 
 
 def solution(mesh):

time: 106 us -> 96.7 us (0.912)
  Pallas kernels: 102 us -> 92.5 us
  other arithmetic: 0 us -> 2.31 us
  local copies, waits for them, and re-layouts: 2.78 us -> 0.52 us
    pallas_call x1, Pallas kernels: 102 us -> 92.5 us  [body(): pl.pallas_call(functools.partial(kernel, sectors, ny, nz), out_shape=(jax...]
    mul x0 -> x1, other arithmetic: none -> 2.31 us  [body(): return (vector * math.sqrt(float(B * B * sectors)), energies)]
    unnamed x4 -> x3, local copies, waits for them, and re-layouts: 2.78 us -> 0.52 us
where the time goes in v2:
time: 96.7 us; the launch traced here: 96.6 us
  Pallas kernels  92.5 us (96%)
  other arithmetic  2.31 us (2%)
  between operations  1.29 us (1%)
    pallas_call x1, Pallas kernels, body(): pl.pallas_call(functools.partial(kernel, sectors, ny, nz), out_shape=(jax...  92.5 us
    mul x1, other arithmetic, body(): return (vector * math.sqrt(float(B * B * sectors)), energies)  2.31 us

profile of v2, /device:TPU:32, one launch (start us, length us, event | category | flops | bytes accessed | tf_op | source)
XLA Modules:
  0.0 96.6 jit_solution(11920408858453920822)
XLA Ops:
  1.3 92.5 %davidson.1 = (f32[512,512]{1,0:T(8,128)}, f32[3]{0:T(128)}) custom-call(bf16[1,2,512,512]{3,2,1,0:T(8,128)(2,1)} %left.1, bf16[1,2,512,512]{3,2,1,0:T(8,128)(2,1)} %right.1, f32[512,512]{1,0:T(8,128)} %guess.1, f32[512,512]{1,0:T(8,128)} %precond.1, s32[1]{0:T(128)S(6)} %copy.8.used_ref), custom_call_target="tpu_custom_call" | custom-call | tf_op jit(solution)/shard_map/davidson/pallas_call | solution.py:539
  93.8 0.0 copy-start
  93.8 2.3 %broadcast_multiply_fusion = f32[512,512]{1,0:T(8,128)} fusion(f32[512,512]{1,0:T(8,128)} %get-tuple-element.4), kind=kLoop, calls=%fused_computation | loop fusion | flops 262144 | bytes 2097152 | tf_op jit(solution)/shard_map/mul | solution.py:550
  96.1 0.0 copy-done
  96.1 0.5 copy.9
Async XLA Ops:
  93.8 2.3 %copy-start = (f32[3]{0:T(128)S(1)}, f32[3]{0:T(128)}, u32[]{:S(2)}) copy-start(f32[3]{0:T(128)} %get-tuple-element.9) | copy-start | bytes 40

commit v3 on v2

--- a/solution.py
+++ b/solution.py
@@ -42,12 +42,12 @@
     kw, kw16, kup, xsend,
     x, h, t, xu, hu, tu, tb, tub,
     gown, gup, so, sr, ro, rr,
-    acc, praise, in1, inn, keep_own,
-    sc_c, sc_x, sc_y, sc_z, coef,
+    acc, praise, in1, inn, keep_own, staged,
+    sc_x, sc_y, sc_z, sc_t, coef,
     load_sem, env_s, env_r, k_s, k_r,
     up_s, up_r, upc_s, upc_r, own_s, own_r, ownc_s, ownc_r,
     so_s, ro_r, sr_s, rr_r,
-    scc_s, scc_r, scx_s, scx_r, scy_s, scy_r, scz_s, scz_r,
+    scx_s, scx_r, scy_s, scy_r, scz_s, scz_r, sct_s, sct_r,
 ):
     g = lax.axis_index("grp")
     s = lax.axis_index("sec")
@@ -63,8 +63,10 @@
     def xdev(j, sec):
         return (j * 2 + c, sec)
 
+    xs = [lax.rem(px + k, NX) for k in range(NX)]
+
     def xoff(k):
-        return lax.rem(px + k, NX)
+        return xs[k % NX]
 
     def rcopy(src, dst, ssem, rsem, dev):
         return pltpu.make_async_remote_copy(
@@ -88,13 +90,18 @@
         local[i].start()
 
     barrier = pltpu.get_barrier_semaphore()
-    peers = [partner]
-    peers += [xdev(xoff(k), s) for k in range(1, NX)]
-    peers += [(g, above), (g, below)]
-    peers += [(g, lax.rem(py + k, ny) * nz + pz) for k in range(1, ny)]
-    peers += [(g, py * nz + lax.rem(pz + k, nz)) for k in range(1, nz)]
-    for peer in peers:
+    rows_y = [(px * 2 + 1, lax.rem(py + k, ny) * nz + pz) for k in range(1, ny)]
+    column = [(px * 2 + 1, py * nz + lax.rem(pz + k, nz)) for k in range(1, nz)]
+    shared = [partner]
+    shared += [(xs[k] * 2 + core, s) for k in range(1, NX) for core in range(2)]
+    shared += [(g, above), (g, below)]
+    for peer in shared:
         pl.semaphore_signal(barrier, inc=1, device_id=peer, device_id_type=MESH)
+
+    @pl.when(c == 1)
+    def _():
+        for peer in rows_y + column:
+            pl.semaphore_signal(barrier, inc=1, device_id=peer, device_id_type=MESH)
 
     used = used_ref[0]
     row_ids = lax.broadcasted_iota(jnp.int32, (Q, HALF), 0)
@@ -118,15 +125,20 @@
         return 0
 
     lax.fori_loop(0, NX, start_rows, 0)
-    pl.semaphore_wait(barrier, len(peers))
-
-    def up_start(j, _):
+
+    @pl.when(c == 1)
+    def _():
+        pl.semaphore_wait(barrier, len(shared + rows_y + column))
+
+    @pl.when(c == 0)
+    def _():
+        pl.semaphore_wait(barrier, len(shared))
+
+
+    for j in range(NX):
         rcopy(
             xsend.at[c, rows_of(j)], gup.at[0, c, rows_of(j)], up_s.at[0, j], up_r.at[0, j], (g, below)
         ).start()
-        return 0
-
-    lax.fori_loop(0, NX, up_start, 0)
     envs = [
         (left.at[0, 1], lr.at[:, 512:1024]),
         (right.at[0, 1, :, theirs], rt.at[:, 256:512]),
@@ -179,59 +191,60 @@
             kw16[half] = kw[half].astype(BF16)
         k_copy.start()
 
-    def upper_forward(r):
-        def one(j, _):
-            rcopy(
-                gup.at[r, c, rows_of(j)], gup.at[r, c, rows_of(j)], up_s.at[r, j], up_r.at[r, j], partner
-            ).wait_recv()
-            rcopy(
-                gup.at[r, c, rows_of(j)], gup.at[r, c, rows_of(j)], upc_s.at[r, j], upc_r.at[r, j], partner
-            ).start()
-            return 0
-
-        lax.fori_loop(0, NX, one, 0)
-
-    def upper_update(r):
-        def wait(j):
-            rcopy(
-                gup.at[r, c, rows_of(j)], gup.at[r, other, rows_of(j)], upc_s.at[r, j], upc_r.at[r, j], partner
-            ).wait_recv()
+    def upper_arrive(r, forward):
+        for k in (0, 1, 3, 2):
+            j = xoff(k)
+            there = gup.at[r, c, rows_of(j)]
+            rcopy(there, there, up_s.at[r, j], up_r.at[r, j], partner).wait_recv()
+            if forward:
+                rcopy(there, there, upc_s.at[r, j], upc_r.at[r, j], partner).start()
+
+    def upper_wait(r, j):
+        rcopy(
+            gup.at[r, c, rows_of(j)], gup.at[r, other, rows_of(j)], upc_s.at[r, j], upc_r.at[r, j], partner
+        ).wait_recv()
+
+    def upper_half(r, half, exchanged):
+        columns = slice(half * HALF, (half + 1) * HALF)
 
         @pl.when(r == 0)
         def _():
-            def one(j, _):
-                wait(j)
-                for half in range(2):
-                    got = gup[0, half, rows_of(j)]
-                    tub[rows_of(j), half * HALF : (half + 1) * HALF] = got
-                    tu[half, rows_of(j)] = got.astype(F32)
-                    xu[half, rows_of(j)] = jnp.zeros((Q, HALF), F32)
-                    hu[half, rows_of(j)] = jnp.zeros((Q, HALF), F32)
-                return 0
-
-            lax.fori_loop(0, NX, one, 0)
-
+            for k in (0, 1, 3, 2):
+                j = xoff(k)
+                if exchanged:
+                    upper_wait(r, j)
+                got = gup[0, half, rows_of(j)]
+                tub[rows_of(j), columns] = got
+                tu[half, rows_of(j)] = got.astype(F32)
+                xu[half, rows_of(j)] = jnp.zeros((Q, HALF), F32)
+                hu[half, rows_of(j)] = jnp.zeros((Q, HALF), F32)
+
+        @pl.when(r > 0)
+        def _():
+            a0, d0, ritz = coef[0], coef[1], coef[2]
+            for k in (0, 1, 3, 2):
+                j = xoff(k)
+                if exchanged:
+                    upper_wait(r, j)
+                new_x = a0 * xu[half, rows_of(j)] + d0 * tu[half, rows_of(j)]
+                new_h = a0 * hu[half, rows_of(j)] + d0 * gup[r, half, rows_of(j)].astype(F32)
+                new_t = kup[half, rows_of(j)].astype(F32) * (new_h - ritz * new_x)
+                xu[half, rows_of(j)] = new_x
+                hu[half, rows_of(j)] = new_h
+                tu[half, rows_of(j)] = new_t
+                tub[rows_of(j), columns] = new_t.astype(BF16)
+
+    def upper_own(r):
+        for half in range(2):
+            pl.when(c == half)(functools.partial(upper_half, r, half, False))
+
+    def upper_other(r):
         @pl.when(r == 1)
         def _():
             rcopy(kup.at[other], kup.at[other], k_s.at[1], k_r.at[1], partner).wait_recv()
 
-        @pl.when(r > 0)
-        def _():
-            a0, d0, ritz = coef[0], coef[1], coef[2]
-
-            def one(j, _):
-                wait(j)
-                for half in range(2):
-                    new_x = a0 * xu[half, rows_of(j)] + d0 * tu[half, rows_of(j)]
-                    new_h = a0 * hu[half, rows_of(j)] + d0 * gup[r, half, rows_of(j)].astype(F32)
-                    new_t = kup[half, rows_of(j)].astype(F32) * (new_h - ritz * new_x)
-                    xu[half, rows_of(j)] = new_x
-                    hu[half, rows_of(j)] = new_h
-                    tu[half, rows_of(j)] = new_t
-                    tub[rows_of(j), half * HALF : (half + 1) * HALF] = new_t.astype(BF16)
-                return 0
-
-            lax.fori_loop(0, NX, one, 0)
+        for half in range(2):
+            pl.when(other == half)(functools.partial(upper_half, r, half, True))
 
     def local_sums(extra):
         xb, tv, hb = x[c, rows_of(px)], t[c, rows_of(px)], h[c, rows_of(px)]
@@ -243,35 +256,90 @@
             axis=0,
         )
 
-    def stage(buf, ssem, rsem, size, me, dev_of):
-        def send(r, value):
-            buf[r, me] = value
-            for k in range(1, size):
-                rcopy(
-                    buf.at[r, me], buf.at[r, me], ssem.at[r, k], rsem.at[r, me], dev_of(lax.rem(me + k, size))
-                ).start()
-
-        def finish(r):
-            for k in range(1, size):
-                src = lax.rem(me + k, size)
-                rcopy(buf.at[r, me], buf.at[r, src], ssem.at[r, k], rsem.at[r, src], dev_of(src)).wait_recv()
-            total = buf[r, 0]
-            for k in range(1, size):
-                total = total + buf[r, k]
-            return total
-
-        def drain(r):
-            for k in range(1, size):
-                rcopy(
-                    buf.at[r, me], buf.at[r, me], ssem.at[r, k], rsem.at[r, me], dev_of(lax.rem(me + k, size))
-                ).wait_send()
-
-        return send, finish, drain
-
-    c_send, c_finish, c_drain = stage(sc_c, scc_s, scc_r, 2, c, lambda i: (px * 2 + i, s))
-    x_send, x_finish, x_drain = stage(sc_x, scx_s, scx_r, NX, px, lambda i: (i * 2 + c, s))
-    y_send, y_finish, y_drain = stage(sc_y, scy_s, scy_r, ny, py, lambda i: (g, i * nz + pz))
-    z_send, z_finish, z_drain = stage(sc_z, scz_s, scz_r, nz, pz, lambda i: (g, py * nz + i))
+    y_slots = [lax.rem(py + k, ny) for k in range(ny)]
+    z_slots = [lax.rem(pz + k, nz) for k in range(nz)]
+    my_slot = px * 2 + c
+
+    def x_copy(r, k, slot):
+        return rcopy(sc_x.at[r, slot], sc_x.at[r, slot], scx_s.at[r, k], scx_r.at[r, slot], (xs[k] * 2 + 1, s))
+
+    def y_copy(r, k, slot):
+        return rcopy(sc_y.at[r, slot], sc_y.at[r, slot], scy_s.at[r, k], scy_r.at[r, slot], rows_y[k - 1])
+
+    def z_copy(r, k, slot):
+        return rcopy(sc_z.at[r, slot], sc_z.at[r, slot], scz_s.at[r, k], scz_r.at[r, slot], column[k - 1])
+
+    def t_copy(r):
+        return rcopy(sc_t.at[r], sc_t.at[r], sct_s.at[r], sct_r.at[r], partner)
+
+    def added(buf, r, size):
+        total = buf[r, 0]
+        for k in range(1, size):
+            total = total + buf[r, k]
+        return total
+
+    def sums_out(r, value):
+        sc_x[r, my_slot] = value
+        for k in (2, 1, 3):
+            x_copy(r, k, my_slot).start()
+
+        @pl.when(c == 0)
+        def _():
+            x_copy(r, 0, my_slot).start()
+
+    def rows_out(r):
+        @pl.when(c == 1)
+        def _():
+            for k in range(NX):
+                x_copy(r, k, xs[k] * 2).wait_recv()
+                if k:
+                    x_copy(r, k, xs[k] * 2 + 1).wait_recv()
+            sc_y[r, py] = added(sc_x, r, 2 * NX)
+            for k in range(1, ny):
+                y_copy(r, k, py).start()
+
+    def column_out(r):
+        @pl.when(c == 1)
+        def _():
+            for k in range(1, ny):
+                y_copy(r, k, y_slots[k]).wait_recv()
+            sc_z[r, pz] = added(sc_y, r, ny)
+            for k in range(1, nz):
+                z_copy(r, k, pz).start()
+
+    def total_out(r):
+        @pl.when(c == 1)
+        def _():
+            for k in range(1, nz):
+                z_copy(r, k, z_slots[k]).wait_recv()
+            sc_t[r] = added(sc_z, r, nz)
+            t_copy(r).start()
+
+        @pl.when(c == 0)
+        def _():
+            t_copy(r).wait_recv()
+
+        return sc_t[r]
+
+    def sums_drain(r):
+        for k in range(1, NX):
+            x_copy(r, k, my_slot).wait_send()
+
+        @pl.when(c == 0)
+        def _():
+            x_copy(r, 0, my_slot).wait_send()
+
+        @pl.when(c == 1)
+        def _():
+            for k in range(1, ny):
+                y_copy(r, k, py).wait_send()
+
+    def column_drain(r):
+        @pl.when(c == 1)
+        def _():
+            for k in range(1, nz):
+                z_copy(r, k, pz).wait_send()
+            t_copy(r).wait_send()
 
     def coefficients(total, r, ritz):
         sums = jnp.sum(total, axis=1, keepdims=True)
@@ -309,21 +377,19 @@
         raise_inner()
         praise[...] = dot(lr[...], in1[...])
 
-        def raise_rows(k, _):
-            j = xoff(k + 2)
+        for k in (2, 3, 1, 0):
+            j = xoff(k)
             sr[r, rows_of(j)] = praise[rows_of(j)].astype(BF16)
             rcopy(sr.at[r, rows_of(j)], rr.at[r, rows_of(j)], sr_s.at[r, j], rr_r.at[r, j], (g, above)).start()
-            return 0
-
-        lax.fori_loop(0, NX, raise_rows, 0)
 
         @pl.when(r == 0)
         def _():
             ready_own()
+            ready_lower()
 
         for k in range(4):
             inn[k * 512 : (k + 1) * 512] = dot(tb[...], rt[:, 512 + k * 256 : 768 + k * 256]).astype(BF16)
-        upper_forward(r)
+        upper_arrive(r, True)
         acc[...] = dot(lo[:, 0:2048], inn[0:2048])
 
         def own_part(j, total):
@@ -331,17 +397,14 @@
 
         part = lax.fori_loop(0, NX, own_part, jnp.zeros((1, 128), F32))
 
-        @pl.when(r == 0)
-        def _():
-            ready_lower()
-
-        upper_update(r)
+        upper_own(r)
 
         def raise_part(j, total):
             return total + 2.0 * fold(praise[rows_of(j)] * tu[c, rows_of(j)])
 
         part = lax.fori_loop(0, NX, raise_part, part)
-        c_send(r, local_sums(part))
+        sums_out(r, local_sums(part))
+        upper_other(r)
 
         @pl.when(r == 0)
         def _():
@@ -350,33 +413,24 @@
         for k in range(2):
             inn[2048 + k * 512 : 2560 + k * 512] = dot(tub[...], ru[:, k * 256 : (k + 1) * 256]).astype(BF16)
         acc[...] += dot(lo[:, 2048:3072], inn[2048:3072])
-        x_send(r, c_finish(r))
-
-        def send_rows(k, _):
-            j = xoff(k + 2)
+
+        for k in (2, 3, 1, 0):
+            if k == 0:
+                rows_out(r)
+            j = xoff(k)
             rcopy(sr.at[r, rows_of(j)], rr.at[r, rows_of(j)], sr_s.at[r, j], rr_r.at[r, j], (g, above)).wait_recv()
             value = acc[rows_of(j)] + rr[r, rows_of(j)].astype(F32)
 
-            @pl.when(j == px)
-            def _():
+            if k == 0:
                 keep_own[...] = value
-
-            @pl.when(j != px)
-            def _():
+            else:
                 so[r, rows_of(j)] = value.astype(BF16)
                 rcopy(so.at[r, rows_of(j)], ro.at[r, px], so_s.at[r, j], ro_r.at[r, px], xdev(j, s)).start()
 
-            return 0
-
-        lax.fori_loop(0, NX, send_rows, 0)
-
-        def own_in(k, _):
+        column_out(r)
+        for k in range(1, NX):
             j = xoff(k)
             rcopy(so.at[r, rows_of(j)], ro.at[r, j], so_s.at[r, j], ro_r.at[r, j], xdev(j, s)).wait_recv()
-            return 0
-
-        y_send(r, x_finish(r))
-        lax.fori_loop(1, NX, own_in, 0)
         value = keep_own[...]
         for k in range(1, NX):
             value = value + ro[r, xoff(k)].astype(F32)
@@ -395,7 +449,6 @@
             k_copy.wait_recv()
             k_forward.start()
 
-        z_send(r, y_finish(r))
 
         for k in (1, 3, 2):
             j = xoff(k)
@@ -404,7 +457,7 @@
             rcopy(there, there, ownc_s.at[r, j], ownc_r.at[r, j], partner).start()
             rcopy(there, gup.at[r + 1, c, rows_of(j)], up_s.at[r + 1, j], up_r.at[r + 1, j], (g, below)).start()
 
-        new_ritz = set_coef(z_finish(r), r, ritz)
+        new_ritz = set_coef(total_out(r), r, ritz)
 
         @pl.when(r > 0)
         def _():
@@ -412,7 +465,7 @@
 
         a0, d0, theta = coef[0], coef[1], coef[2]
 
-        def update(k, _):
+        for k in range(NX):
             j = xoff(k)
             there = gown.at[r, other, rows_of(j)]
             rcopy(there, there, ownc_s.at[r, j], ownc_r.at[r, j], partner).wait_recv()
@@ -424,9 +477,6 @@
                 h[half, rows_of(j)] = new_h
                 t[half, rows_of(j)] = new_t
                 tb[rows_of(j), half * HALF : (half + 1) * HALF] = new_t.astype(BF16)
-            return 0
-
-        lax.fori_loop(0, NX, update, 0)
         return new_ritz
 
     ritz = lax.fori_loop(0, ITERS, round_body, jnp.zeros((1, 1), F32))
@@ -436,7 +486,7 @@
     inn[0:512] = dot(tb[...], rt[:, 512:768]).astype(BF16)
     inn[512:1024] = dot(tb[...], rt[:, 768:1024]).astype(BF16)
 
-    upper_forward(last)
+    upper_arrive(last, False)
     praise[...] = dot(lr[...], in1[...])
     acc[...] = dot(lo[:, 0:1024], inn[0:1024])
 
@@ -444,69 +494,68 @@
         return part + 2.0 * fold(acc[rows_of(j)] * t[c, rows_of(j)])
 
     part = lax.fori_loop(0, NX, last_own, jnp.zeros((1, 128), F32))
-    upper_update(last)
+    upper_own(last)
 
     def last_part(j, total):
         return total + 2.0 * fold(praise[rows_of(j)] * tu[c, rows_of(j)])
 
     part = lax.fori_loop(0, NX, last_part, part)
-    c_send(last, local_sums(part))
-    x_send(last, c_finish(last))
+    sums_out(last, local_sums(part))
 
     def drain_round(r, _):
-        def rows(j, _):
+        for j in range(NX):
             rcopy(sr.at[r, rows_of(j)], rr.at[r, rows_of(j)], sr_s.at[r, j], rr_r.at[r, j], (g, above)).wait_send()
             home = gown.at[r, c, rows_of(px)]
             rcopy(home, home, ownc_s.at[r, j], ownc_r.at[r, px], partner).wait_send()
-            return 0
-
-        def others(k, _):
+        for k in range(1, NX):
             j = xoff(k)
             rcopy(so.at[r, rows_of(j)], ro.at[r, px], so_s.at[r, j], ro_r.at[r, px], xdev(j, s)).wait_send()
-            home = gown.at[r, c, rows_of(px)]
             rcopy(home, home, own_s.at[r, k], own_r.at[r, px], xdev(j, s)).wait_send()
-            return 0
-
-        lax.fori_loop(0, NX, rows, 0)
-        lax.fori_loop(1, NX, others, 0)
         return 0
 
     def drain_upper(r, _):
-        def rows(j, _):
+        for j in range(NX):
             there = gup.at[r, c, rows_of(j)]
             rcopy(there, there, up_s.at[r, j], up_r.at[r, j], (g, below)).wait_send()
-            rcopy(there, there, upc_s.at[r, j], upc_r.at[r, j], partner).wait_send()
-            return 0
-
-        lax.fori_loop(0, NX, rows, 0)
+
+            @pl.when(r < ITERS)
+            def _():
+                rcopy(there, there, upc_s.at[r, j], upc_r.at[r, j], partner).wait_send()
+
         return 0
 
+    def drain_sums(r, _):
+        sums_drain(r)
+        column_drain(r)
+        return 0
+
     lax.fori_loop(0, ITERS, drain_round, 0)
+    rows_out(last)
     lax.fori_loop(0, ITERS + 1, drain_upper, 0)
     for copy in env:
         copy.wait_send()
     k_copy.wait_send()
     k_forward.wait_send()
 
-    y_send(last, x_finish(last))
-    z_send(last, y_finish(last))
-    set_coef(z_finish(last), last, ritz)
+    column_out(last)
+    lax.fori_loop(0, ITERS, drain_sums, 0)
+    sums_drain(last)
+    set_coef(total_out(last), last, ritz)
     energies[last - 1] = coef[2]
     a0, d0 = coef[0], coef[1]
 
-    def write(j, _):
+    writes = []
+    for j in range(NX):
         for half in range(2):
-            out[rows_of(j), half * HALF : (half + 1) * HALF] = a0 * x[half, rows_of(j)] + d0 * t[half, rows_of(j)]
-        return 0
-
-    lax.fori_loop(0, NX, write, 0)
-
-    def drain_sums(r, _):
-        for drain in (c_drain, x_drain, y_drain, z_drain):
-            drain(r)
-        return 0
-
-    lax.fori_loop(0, ITERS + 1, drain_sums, 0)
+            staged[rows_of(j), half * HALF : (half + 1) * HALF] = (
+                a0 * x[half, rows_of(j)] + d0 * t[half, rows_of(j)]
+            )
+        writes.append(pltpu.make_async_copy(staged.at[rows_of(j)], out.at[rows_of(j)], load_sem.at[j]))
+        writes[-1].start()
+
+    column_drain(last)
+    for copy in writes:
+        copy.wait()
 
 
 def body(left_env, right_env, guess, precond, sector_rows):
@@ -524,23 +573,23 @@
         vm((ITERS,) + halves, BF16), vm((rounds,) + halves, BF16),
         vm((ITERS, B, HALF), BF16), vm((ITERS, B, HALF), BF16),
         vm((ITERS, NX, Q, HALF), BF16), vm((ITERS, B, HALF), BF16),
-        vm((B, HALF), F32), vm((B, HALF), F32), vm((1024, HALF), BF16), vm((3072, HALF), BF16), vm((Q, HALF), F32),
-        vm((rounds, 2, 8, 128), F32), vm((rounds, NX, 8, 128), F32),
-        vm((rounds, ny, 8, 128), F32), vm((rounds, nz, 8, 128), F32),
+        vm((B, HALF), F32), vm((B, HALF), F32), vm((1024, HALF), BF16), vm((3072, HALF), BF16), vm((Q, HALF), F32), vm((B, B), F32),
+        vm((rounds, 2 * NX, 8, 128), F32), vm((rounds, ny, 8, 128), F32),
+        vm((rounds, nz, 8, 128), F32), vm((rounds, 8, 128), F32),
         pltpu.SMEM((4,), F32),
         dma((10,)), dma((6,)), dma((6,)), dma((2,)), dma((2,)),
         dma((rounds, NX)), dma((rounds, NX)), dma((rounds, NX)), dma((rounds, NX)),
         dma((ITERS, NX)), dma((ITERS, NX)), dma((ITERS, NX)), dma((ITERS, NX)),
         dma((ITERS, NX)), dma((ITERS, NX)), dma((ITERS, NX)), dma((ITERS, NX)),
-        dma((rounds, 2)), dma((rounds, 2)), dma((rounds, NX)), dma((rounds, NX)),
-        dma((rounds, ny)), dma((rounds, ny)), dma((rounds, nz)), dma((rounds, nz)),
+        dma((rounds, NX)), dma((rounds, 2 * NX)), dma((rounds, ny)), dma((rounds, ny)),
+        dma((rounds, nz)), dma((rounds, nz)), dma((rounds,)), dma((rounds,)),
     ]
     any_space = pl.BlockSpec(memory_space=pl.ANY)
     vector, energies = pl.pallas_call(
         functools.partial(kernel, sectors, ny, nz),
         out_shape=(jax.ShapeDtypeStruct((B, B), F32), jax.ShapeDtypeStruct((ITERS,), F32)),
         in_specs=[any_space] * 4 + [pl.BlockSpec(memory_space=pltpu.SMEM)],
-        out_specs=(pl.BlockSpec(memory_space=pltpu.VMEM), pl.BlockSpec(memory_space=pltpu.SMEM)),
+        out_specs=(pl.BlockSpec(memory_space=pl.ANY), pl.BlockSpec(memory_space=pltpu.SMEM)),
         scratch_shapes=scratch,
         compiler_params=pltpu.CompilerParams(
             collective_id=0, has_side_effects=True, vmem_limit_bytes=56 * 1024 * 1024

time: 96.7 us -> 95.7 us (0.990)
  Pallas kernels: 92.5 us -> 90.7 us
    pallas_call x1, Pallas kernels: 92.5 us -> 90.7 us  [body(): pl.pallas_call(functools.partial(kernel, sectors, ny, nz), out_shape=(jax...]
where the time goes in v3:
time: 95.7 us; the launch traced here: 94.8 us
  Pallas kernels  90.7 us (95%)
  other arithmetic  2.31 us (2%)
  between operations  1.29 us (1%)
    pallas_call x1, Pallas kernels, body(): pl.pallas_call(functools.partial(kernel, sectors, ny, nz), out_shape=(jax...  90.7 us
    mul x1, other arithmetic, body(): return (vector * math.sqrt(float(B * B * sectors)), energies)  2.31 us

profile of v3, /device:TPU:32, one launch (start us, length us, event | category | flops | bytes accessed | tf_op | source)
XLA Modules:
  0.0 94.8 jit_solution(9228231963853744658)
XLA Ops:
  1.3 90.7 %davidson.1 = (f32[512,512]{1,0:T(8,128)}, f32[3]{0:T(128)}) custom-call(bf16[1,2,512,512]{3,2,1,0:T(8,128)(2,1)} %left.1, bf16[1,2,512,512]{3,2,1,0:T(8,128)(2,1)} %right.1, f32[512,512]{1,0:T(8,128)} %guess.1, f32[512,512]{1,0:T(8,128)} %precond.1, s32[1]{0:T(128)S(6)} %copy.8.used_ref), custom_call_target="tpu_custom_call" | custom-call | tf_op jit(solution)/shard_map/davidson/pallas_call | solution.py:588
  92.0 0.0 copy-start
  92.0 2.3 %broadcast_multiply_fusion = f32[512,512]{1,0:T(8,128)} fusion(f32[512,512]{1,0:T(8,128)} %get-tuple-element.4), kind=kLoop, calls=%fused_computation | loop fusion | flops 262144 | bytes 2097152 | tf_op jit(solution)/shard_map/mul | solution.py:599
  94.3 0.0 copy-done
  94.3 0.5 copy.9
Async XLA Ops:
  92.0 2.3 %copy-start = (f32[3]{0:T(128)S(1)}, f32[3]{0:T(128)}, u32[]{:S(2)}) copy-start(f32[3]{0:T(128)} %get-tuple-element.9) | copy-start | bytes 40

commit v4 on v3

--- a/solution.py
+++ b/solution.py
@@ -295,7 +295,7 @@
                 if k:
                     x_copy(r, k, xs[k] * 2 + 1).wait_recv()
             sc_y[r, py] = added(sc_x, r, 2 * NX)
-            for k in range(1, ny):
+            for k in sorted(range(1, ny), key=lambda k: -min(k, ny - k)):
                 y_copy(r, k, py).start()
 
     def column_out(r):
@@ -304,7 +304,7 @@
             for k in range(1, ny):
                 y_copy(r, k, y_slots[k]).wait_recv()
             sc_z[r, pz] = added(sc_y, r, ny)
-            for k in range(1, nz):
+            for k in sorted(range(1, nz), key=lambda k: -min(k, nz - k)):
                 z_copy(r, k, pz).start()
 
     def total_out(r):
@@ -389,8 +389,10 @@
 
         for k in range(4):
             inn[k * 512 : (k + 1) * 512] = dot(tb[...], rt[:, 512 + k * 256 : 768 + k * 256]).astype(BF16)
-        upper_arrive(r, True)
+        pl.when(c == 1)(functools.partial(upper_arrive, r, True))
         acc[...] = dot(lo[:, 0:2048], inn[0:2048])
+
+        pl.when(c == 0)(functools.partial(upper_arrive, r, True))
 
         def own_part(j, total):
             return total + fold(acc[rows_of(j)] * t[c, rows_of(j)])

time: 95.7 us -> 95.1 us (level)
  Pallas kernels: 90.7 us -> 89.7 us
    pallas_call x1, Pallas kernels: 90.7 us -> 89.7 us  [body(): pl.pallas_call(functools.partial(kernel, sectors, ny, nz), out_shape=(jax...]
where the time goes in v4:
time: 95.1 us; the launch traced here: 93.9 us
  Pallas kernels  89.7 us (94%)
  other arithmetic  2.31 us (2%)
  between operations  1.29 us (1%)
    pallas_call x1, Pallas kernels, body(): pl.pallas_call(functools.partial(kernel, sectors, ny, nz), out_shape=(jax...  89.7 us
    mul x1, other arithmetic, body(): return (vector * math.sqrt(float(B * B * sectors)), energies)  2.31 us

profile of v4, /device:TPU:32, one launch (start us, length us, event | category | flops | bytes accessed | tf_op | source)
XLA Modules:
  0.0 93.9 jit_solution(15939991951845939851)
XLA Ops:
  1.3 89.7 %davidson.1 = (f32[512,512]{1,0:T(8,128)}, f32[3]{0:T(128)}) custom-call(bf16[1,2,512,512]{3,2,1,0:T(8,128)(2,1)} %left.1, bf16[1,2,512,512]{3,2,1,0:T(8,128)(2,1)} %right.1, f32[512,512]{1,0:T(8,128)} %guess.1, f32[512,512]{1,0:T(8,128)} %precond.1, s32[1]{0:T(128)S(6)} %copy.8.used_ref), custom_call_target="tpu_custom_call" | custom-call | tf_op jit(solution)/shard_map/davidson/pallas_call | solution.py:590
  91.0 0.0 copy-start
  91.0 2.3 %broadcast_multiply_fusion = f32[512,512]{1,0:T(8,128)} fusion(f32[512,512]{1,0:T(8,128)} %get-tuple-element.4), kind=kLoop, calls=%fused_computation | loop fusion | flops 262144 | bytes 2097152 | tf_op jit(solution)/shard_map/mul | solution.py:601
  93.3 0.0 copy-done
  93.4 0.5 copy.9
Async XLA Ops:
  91.0 2.3 %copy-start = (f32[3]{0:T(128)S(1)}, f32[3]{0:T(128)}, u32[]{:S(2)}) copy-start(f32[3]{0:T(128)} %get-tuple-element.9) | copy-start | bytes 40
